TPU v7x, 128 devices: a whole 4x4x4 slice. The times are simulated.
128 devices in a mesh: ctx: 32 (over z, x, core), head: 4 (over y).
Axes of the slice: x: 4, y: 4, z: 4, core: 2. Of those that a mesh axis runs over, the one named last changes fastest.
Arguments:
- queries: bfloat16 [8192, 4096], P('ctx', 'head'), may hold values from -6 to 6
- key_rows: bfloat16 [8192, 4096], P('ctx', 'head'), may hold values from -6 to 6
- value_rows: bfloat16 [8192, 4096], P('ctx', 'head'), may hold values from -6 to 6
- norm_gain: float32 [4096], P('head'), may hold values from 0.25 to 1.75
- out_weight: bfloat16 [4096, 6144], P('head'), may hold values from -0.09375 to 0.09375
- out_cotangent: bfloat16 [8192, 6144], P(('ctx', 'head')), may hold values from -6 to 6
Outputs:
- layer_out: bfloat16 [8192, 6144], P(('ctx', 'head'))
- query_grad: bfloat16 [8192, 4096], P('ctx', 'head')
- key_grad: bfloat16 [8192, 4096], P('ctx', 'head')
- value_grad: bfloat16 [8192, 4096], P('ctx', 'head')
All inputs are finite; a program needn't handle non-finite values.
Results may differ from a plain program's by a relative error of at most 0.0065.
Values may be sent and summed in bfloat16 or wider, within the bound.
A program may use at most 128 MiB of HBM per device.

v0:
```python
import jax
import jax.numpy as jnp
from jax import lax
from jax.sharding import PartitionSpec as P

DH = 128


def normalize(hidden, gain):
    scale = lax.rsqrt(jnp.mean(hidden * hidden, axis=-1, keepdims=True) + 1e-06)
    return hidden * scale * gain


def per_device(queries, key_rows, value_rows, norm_gain, out_weight, out_cotangent):
    block_len = queries.shape[0]
    local_heads = queries.shape[1] // DH
    shape = (block_len, local_heads, DH)
    query_blocks = queries.reshape(shape)
    key_blocks = key_rows.reshape(shape)
    value_blocks = value_rows.reshape(shape)
    gain = norm_gain.reshape(local_heads, DH)
    position = lax.axis_index("ctx")
    causal = jnp.arange(block_len)[:, None] >= jnp.arange(block_len)[None, :]
    f32 = jnp.float32
    bf16 = jnp.bfloat16
    block_state = jnp.einsum(
        "thd,the->hde", key_blocks, value_blocks, preferred_element_type=f32
    ).astype(bf16)
    piece = lax.all_gather(block_state[None], "ctx", axis=0, tiled=True)
    index_rows = jnp.arange(piece.shape[0])
    weights = (index_rows < position).astype(bf16)
    prefix_sum = jnp.einsum("n,nhde->hde", weights, piece, preferred_element_type=f32)
    prefix_state = prefix_sum.astype(bf16)
    scores = jnp.einsum("thd,shd->hts", query_blocks, key_blocks, preferred_element_type=f32)
    inner = jnp.where(causal, scores, 0.0).astype(bf16)
    attn = jnp.einsum("hts,she->the", inner, value_blocks, preferred_element_type=f32)
    attn = attn + jnp.einsum("thd,hde->the", query_blocks, prefix_state, preferred_element_type=f32)
    normed = normalize(attn, gain).astype(bf16).reshape(block_len, local_heads * DH)
    layer_out = lax.psum_scatter(
        jnp.dot(normed, out_weight, preferred_element_type=f32),
        "head",
        scatter_dimension=0,
        tiled=True,
    ).astype(bf16)
    normed_grad = lax.dot_general(
        lax.all_gather(out_cotangent, "head", axis=0, tiled=True),
        out_weight,
        (((1,), (1,)), ((), ())),
        preferred_element_type=f32,
    )
    unused, pullback = jax.vjp(lambda hidden: normalize(hidden, gain), attn)
    attn_grad = pullback(normed_grad.reshape(shape))[0].astype(bf16)
    grad_state = jnp.einsum(
        "thd,the->hde", query_blocks, attn_grad, preferred_element_type=f32
    ).astype(bf16)
    piece = lax.all_gather(grad_state[None], "ctx", axis=0, tiled=True)
    index_rows = jnp.arange(piece.shape[0])
    weights = (index_rows > position).astype(bf16)
    suffix_sum = jnp.einsum("n,nhde->hde", weights, piece, preferred_element_type=f32)
    suffix_state = suffix_sum.astype(bf16)
    inner_grad = jnp.where(
        causal, jnp.einsum("the,she->hts", attn_grad, value_blocks, preferred_element_type=f32), 0.0
    ).astype(bf16)
    query_grad = jnp.einsum("hts,shd->thd", inner_grad, key_blocks, preferred_element_type=f32)
    query_grad = query_grad + jnp.einsum(
        "the,hde->thd", attn_grad, prefix_state, preferred_element_type=f32
    )
    key_grad = jnp.einsum("hts,thd->shd", inner_grad, query_blocks, preferred_element_type=f32)
    key_grad = key_grad + jnp.einsum(
        "the,hde->thd", value_blocks, suffix_state, preferred_element_type=f32
    )
    value_grad = jnp.einsum("hts,the->she", inner, attn_grad, preferred_element_type=f32)
    value_grad = value_grad + jnp.einsum(
        "thd,hde->the", key_blocks, suffix_state, preferred_element_type=f32
    )
    flat = (block_len, local_heads * DH)
    return (
        layer_out,
        query_grad.reshape(flat).astype(bf16),
        key_grad.reshape(flat).astype(bf16),
        value_grad.reshape(flat).astype(bf16),
    )


def solution(mesh):
    in_specs = (
        P("ctx", "head"),
        P("ctx", "head"),
        P("ctx", "head"),
        P("head"),
        P("head", None),
        P(("ctx", "head"), None),
    )
    out_specs = (P(("ctx", "head"), None), P("ctx", "head"), P("ctx", "head"), P("ctx", "head"))
    return jax.shard_map(
        per_device, mesh=mesh, in_specs=in_specs, out_specs=out_specs, check_vma=False
    )
```

profile of v0, /device:TPU:1, one launch (start us, length us, event | category | flops | bytes accessed | tf_op | source)
XLA Modules:
  0.0 266.4 jit_solution(1220564389024454031)
XLA Ops:
  7.2 0.7 all-gather.6.cloned.1.call-update
  8.0 1.1 copy.65
  9.4 2.0 convolution_convert_fusion.1
  11.6 2.5 select_convert_fusion.1
  14.1 2.8 %convolution_bitcast_fusion.5 = f32[256,8,128]{0,2,1:T(8,128)} fusion(bf16[8,256,256]{2,1,0:T(8,128)(2,1)} %select_convert_fusion.1, bf16[256,1024]{1,0:T(8,128)(2,1)} %param.8), kind=kOutput, calls=%fused_computation.16 | convolution fusion | flops 134217728 | bytes 2621440 | tf_op jit(solution)/shard_map/hts,she->the/dot_general | solution.py:36
  16.9 35.6 %all-gather.6.cloned.1.call-done = bf16[256,6144]{1,0:T(8,128)(2,1)} async-done(((bf16[64,6144]{1,0:T(8,128)(2,1)}), bf16[256,6144]{1,0:T(8,128)(2,1)}) %all-gather.6.cloned.1.call-update) | async-done | bytes 3145744 | tf_op jit(solution)/shard_map/all_gather | solution.py:46
  52.5 7.4 %fusion.44 = f32[256,1024]{0,1:T(8,128)S(1)} fusion(bf16[256,6144]{1,0:T(8,128)(2,1)} %all-gather.6.cloned.1.call-done, bf16[1024,6144]{1,0:T(8,128)(2,1)} %param.10), kind=kOutput, calls=%fused_computation.63 | convolution fusion | flops 3221225472 | bytes 16777216 | tf_op jit(solution)/shard_map/dot_general | solution.py:45
  59.9 49.1 %all-gather.8.cloned.1.call-done = bf16[256,128,128]{2,1,0:T(8,128)(2,1)} async-done(((bf16[8,128,128]{2,1,0:T(8,128)(2,1)}), bf16[256,128,128]{2,1,0:T(8,128)(2,1)}) %all-gather.8.cloned.1.call-update) | async-done | bytes 8388624 | tf_op jit(solution)/shard_map/all_gather | solution.py:29
  109.0 8.2 %fusion.2 = f32[1,8,128,128]{3,0,2,1:T(1,128)S(1)} fusion(bf16[32,8,128,128]{3,2,1,0:T(8,128)(2,1)} %bitcast.126, s32[]{:T(128)S(6)} %axis_index.15), kind=kOutput, calls=%fused_computation.2 | convolution fusion | flops 8388640 | bytes 8912900 | tf_op jit(solution)/shard_map/n,nhde->hde/dot_general | solution.py:32
  117.2 0.5 multiply_reduce_fusion
  118.1 10.1 %fusion.43 = f32[256,6144]{1,0:T(8,128)} fusion(bf16[256,1024]{0,1:T(8,128)(2,1)S(1)} %bitcast.131, bf16[1024,6144]{1,0:T(8,128)(2,1)} %param.10), kind=kOutput, calls=%fused_computation.62 | convolution fusion | flops 3221225472 | bytes 19398656 | tf_op jit(solution)/shard_map/dot_general | solution.py:40
  128.7 0.9 copy.44
  129.6 0.5 select_convert_fusion
  130.1 0.5 convolution_bitcast_fusion.4
  131.1 1.0 copy.48
  132.1 2.5 fusion.45
  134.6 1.6 convolution_bitcast_fusion.3
  136.2 55.3 %reduce-scatter.2.cloned.1.call-done = f32[64,6144]{1,0:T(8,128)} async-done(((f32[256,6144]{1,0:T(8,128)}), f32[64,6144]{1,0:T(8,128)}) %reduce-scatter.2.cloned.1.call-update) | async-done | bytes 1572880 | tf_op jit(solution)/shard_map/reduce_scatter | solution.py:39
  191.4 2.4 convert_element_type.57
  193.8 53.5 %all-gather.10.cloned.1.call-done = bf16[256,128,128]{2,1,0:T(8,128)(2,1)} async-done(((bf16[8,128,128]{2,1,0:T(8,128)(2,1)}), bf16[256,128,128]{2,1,0:T(8,128)(2,1)}) %all-gather.10.cloned.1.call-update) | async-done | bytes 8388624 | tf_op jit(solution)/shard_map/all_gather | solution.py:56
  247.3 8.2 %fusion = bf16[1,8,128,128]{3,0,2,1:T(2,128)(2,1)S(1)} fusion(bf16[32,8,128,128]{3,2,1,0:T(8,128)(2,1)} %bitcast.125, s32[]{:T(128)S(6)} %axis_index.15), kind=kOutput, calls=%fused_computation | convolution fusion | flops 8388640 | bytes 8650756 | tf_op jit(solution)/shard_map/n,nhde->hde/dot_general | solution.py:59
  255.8 1.7 fusion.9
  257.5 1.0 copy.50
  258.9 1.0 copy.49
  (25 shorter events, 2.6 us)
Async XLA Ops:
  7.2 4.4 %copy-start = (bf16[256,1024]{1,0:T(8,128)(2,1)S(1)}, bf16[256,1024]{1,0:T(8,128)(2,1)}, u32[]{:S(2)}) copy-start(bf16[256,1024]{1,0:T(8,128)(2,1)} %param.6) | copy-start | bytes 1572868
  7.2 45.3 %all-gather.6.cloned.1.call-start = ((), (), s32[]{:S(2)}) async-start(), calls=%async_computation.2 | async-start | bytes 3932160 | tf_op jit(solution)/shard_map/all_gather | solution.py:46
  7.9 101.1 %all-gather.8.cloned.1.call-start = ((), (), s32[]{:S(2)}) async-start(), calls=%async_computation.3 | async-start | bytes 8650752 | tf_op jit(solution)/shard_map/all_gather | solution.py:29
  11.5 179.9 %reduce-scatter.2.cloned.1.call-start = ((), (), s32[]{:S(2)}) async-start(), calls=%async_computation.1 | async-start | bytes 7864320 | tf_op jit(solution)/shard_map/reduce_scatter | solution.py:39
  59.9 57.3 %copy-start.4 = (f32[1024]{0:T(1024)S(1)}, f32[1024]{0:T(1024)}, u32[]{:S(2)}) copy-start(f32[1024]{0:T(1024)} %param.9) | copy-start | bytes 12292
  109.0 8.2 %copy-start.2 = (f32[256,8,128]{0,2,1:T(8,128)S(1)}, f32[256,8,128]{0,2,1:T(8,128)}, u32[]{:S(2)}) copy-start(f32[256,8,128]{0,2,1:T(8,128)} %convolution_bitcast_fusion.5) | copy-start | bytes 3145732
  128.1 1.4 copy-start.1
  128.2 119.1 %all-gather.10.cloned.1.call-start = ((), (), s32[]{:S(2)}) async-start(), calls=%async_computation.4 | async-start | bytes 8650752 | tf_op jit(solution)/shard_map/all_gather | solution.py:56
  130.1 1.0 copy-start.3
Sparse Core Ops, SparseCore 0:
  9.7 42.7 all-gather.5
  55.3 53.6 all-gather.7
  128.3 63.0 reduce-scatter.1
  194.1 53.0 all-gather.9
where the time goes:
time: 267 us; the launch traced here: 266 us
  waiting for transfers between devices  194 us (73%)
  matrix products  49.3 us (18%)
  between operations  13.9 us (5%)
  local copies, waits for them, and re-layouts  5.91 us (2%)
  other arithmetic  2.76 us (1%)
    reduce_scatter x1, waiting for transfers between devices, per_device(): lax.psum_scatter(jnp.dot(normed, out_weight, preferred_element_type=f32),...  55.3 us
    all_gather x1, waiting for transfers between devices, per_device(): piece = lax.all_gather(grad_state[None], 'ctx', axis=0, tiled=True)  53.5 us
    all_gather x1, waiting for transfers between devices, per_device(): piece = lax.all_gather(block_state[None], 'ctx', axis=0, tiled=True)  49.1 us
    all_gather x1, waiting for transfers between devices, per_device(): lax.all_gather(out_cotangent, 'head', axis=0, tiled=True)  35.6 us
    dot_general x2, matrix products, per_device(): jnp.einsum('n,nhde->hde', weights, piece, preferred_element_type=f32)  16.4 us
    dot_general x1, matrix products, per_device(): jnp.dot(normed, out_weight, preferred_element_type=f32)  10.1 us
    dot_general x1, matrix products, per_device(): lax.dot_general(lax.all_gather(out_cotangent, 'head', axis=0, tiled=True)...  7.39 us
  transfers between devices with their start and end apart: 4, of which 4 were waited for; matrix products, arithmetic and copies ran while one was open for 10% of the time, Pallas kernels for 0%

commit v1 on v0

v1 whole, which is shorter than its diff:
```python
import functools

import jax
import jax.numpy as jnp
from jax import lax
from jax.experimental import pallas as pl
from jax.experimental.pallas import tpu as pltpu
from jax.sharding import PartitionSpec as P

DH = 128
MESH = pl.DeviceIdType.MESH
f32 = jnp.float32
bf16 = jnp.bfloat16


def nn(a, b):
    return jnp.dot(a, b, preferred_element_type=f32)


def nt(a, b):
    return lax.dot_general(a, b, (((1,), (1,)), ((), ())), preferred_element_type=f32)


def tn(a, b):
    return lax.dot_general(a, b, (((0,), (0,)), ((), ())), preferred_element_type=f32)


def kernel(
    n_ctx,
    n_head,
    chunk,
    q_hbm,
    k_hbm,
    v_hbm,
    gain,
    w_hbm,
    cot_hbm,
    lo_hbm,
    dq_hbm,
    dk_hbm,
    dv_hbm,
    q,
    k,
    v,
    w,
    cot,
    inner,
    attn,
    scale,
    normed,
    part,
    own,
    p,
    rel,
    fin_dn,
    fin_up,
    ng,
    ag,
    dq,
    dk,
    dv,
    dkb,
    dvb,
    lo,
    st_own,
    st_got,
    st_sum,
    st_pre,
    gs_own,
    gs_got,
    gs_sum,
    gs_suf,
    ld_sem,
    out_sem,
    ag_send,
    ag_recv,
    sc_send,
    sc_recv,
    rel_send,
    rel_recv,
    one_send,
    one_recv,
    two_send,
    two_recv,
):
    c = lax.axis_index("ctx")
    y = lax.axis_index("head")
    up = lax.rem(y + 1, n_head)
    down = lax.rem(y + n_head - 1, n_head)
    far = lax.rem(y + 2, n_head)
    tok, feat = q.shape
    heads = feat // DH
    rows = cot.shape[1]
    width = cot.shape[2]
    n_chunk = width // chunk
    half = rows // 2
    share = st_own.shape[0] // n_ctx

    loads = [
        pltpu.make_async_copy(src, dst, ld_sem.at[i])
        for i, (src, dst) in enumerate(
            ((k_hbm, k), (v_hbm, v), (q_hbm, q), (cot_hbm, cot.at[y]), (w_hbm, w))
        )
    ]
    for load in loads:
        load.start()

    barrier = pltpu.get_barrier_semaphore()

    def greet(i, carry):
        pl.semaphore_signal(
            barrier, inc=1, device_id=(lax.rem(c + i, n_ctx), y), device_id_type=MESH
        )
        return carry

    for near in (up, down):
        pl.semaphore_signal(barrier, inc=1, device_id=(c, near), device_id_type=MESH)
    lax.fori_loop(1, n_ctx, greet, 0)
    pl.semaphore_wait(barrier, n_ctx + 1)

    first, second = pl.ds(0, half), pl.ds(half, half)

    def hop(src, owner, piece, to, i):
        return pltpu.make_async_remote_copy(
            src_ref=src,
            dst_ref=cot.at[owner, piece],
            send_sem=ag_send.at[i],
            recv_sem=ag_recv.at[i],
            device_id=(c, to),
            device_id_type=MESH,
        )

    hops = [
        hop(cot_hbm.at[first], y, first, up, 0),
        hop(cot_hbm.at[second], y, second, down, 3),
        hop(cot_hbm.at[second], y, second, up, 1),
        hop(cot_hbm.at[first], y, first, down, 4),
    ]
    for h in hops:
        h.start()

    def lanes(h):
        return pl.ds(pl.multiple_of(h * DH, DH), DH)

    def piece_of(i):
        return pl.ds(pl.multiple_of(i * share, share), share)

    def exchange(src, dst, i):
        def step(j, carry):
            peer = lax.rem(c + j, n_ctx)
            pltpu.make_async_remote_copy(
                src_ref=src.at[piece_of(peer)],
                dst_ref=dst.at[piece_of(c)],
                send_sem=sc_send.at[i],
                recv_sem=sc_recv.at[i],
                device_id=(peer, y),
                device_id_type=MESH,
            ).start()
            return carry

        lax.fori_loop(1, n_ctx, step, 0)
        dst[piece_of(c), :] = src[piece_of(c), :]

    def exchanged(src, dst, i):
        whole = pl.ds(0, (n_ctx - 1) * share)
        all_of = pltpu.make_async_remote_copy(
            src_ref=src.at[whole],
            dst_ref=dst.at[whole],
            send_sem=sc_send.at[i],
            recv_sem=sc_recv.at[i],
            device_id=(lax.rem(c + 1, n_ctx), y),
            device_id_type=MESH,
        )
        all_of.wait_send()
        all_of.wait_recv()

    loads[0].wait()
    loads[1].wait()

    def state_step(h, carry):
        hs = lanes(h)
        st_own[hs, :] = tn(k[:, hs], v[:, hs]).astype(bf16)
        return carry

    lax.fori_loop(0, heads, state_step, 0)
    exchange(st_own, st_got, 0)

    loads[2].wait()
    causal = lax.broadcasted_iota(jnp.int32, (tok, tok), 0) >= lax.broadcasted_iota(
        jnp.int32, (tok, tok), 1
    )

    def inner_step(h, carry):
        hs = lanes(h)
        masked = jnp.where(causal, nt(q[:, hs], k[:, hs]), 0.0).astype(bf16)
        inner[h] = masked
        attn[:, hs] = nn(masked, v[:, hs])
        return carry

    lax.fori_loop(0, heads, inner_step, 0)

    exchanged(st_own, st_got, 0)

    def prefix_step(i, total):
        st_sum[piece_of(i), :] = total.astype(bf16)
        return total + st_got[piece_of(i), :].astype(f32)

    lax.fori_loop(0, n_ctx, prefix_step, jnp.zeros((share, DH), f32))
    exchange(st_sum, st_pre, 1)
    exchanged(st_sum, st_pre, 1)

    def norm_step(h, carry):
        hs = lanes(h)
        a = attn[:, hs] + nn(q[:, hs], st_pre[hs, :])
        r = lax.rsqrt(jnp.mean(a * a, axis=-1, keepdims=True) + 1e-06)
        x = a * r
        attn[:, hs] = x
        scale[h] = jnp.broadcast_to(r, x.shape)
        normed[:, hs] = (x * gain[:, hs]).astype(bf16)
        return carry

    lax.fori_loop(0, heads, norm_step, 0)

    hops[0].wait_recv()
    onward_up = hop(cot.at[down, first], down, first, up, 2)
    onward_up.start()
    hops[1].wait_recv()
    onward_down = hop(cot.at[up, second], up, second, down, 5)
    onward_down.start()

    loads[4].wait()

    def slab(owner):
        return pl.ds(pl.multiple_of(owner * rows, rows), rows)

    def columns(j):
        return pl.ds(pl.multiple_of(j * chunk, chunk), chunk)

    def relay(j, to):
        return pltpu.make_async_remote_copy(
            src_ref=p.at[slab(far), columns(j)],
            dst_ref=rel.at[:, columns(j)],
            send_sem=rel_send.at[j],
            recv_sem=rel_recv.at[j],
            device_id=(c, to),
            device_id_type=MESH,
        )

    def single(j, to, dst):
        return pltpu.make_async_remote_copy(
            src_ref=p.at[slab(to), columns(j)],
            dst_ref=dst.at[:, columns(j)],
            send_sem=one_send.at[j],
            recv_sem=one_recv.at[j],
            device_id=(c, to),
            device_id_type=MESH,
        )

    def double(j, to, dst):
        return pltpu.make_async_remote_copy(
            src_ref=rel.at[:, columns(j)],
            dst_ref=dst.at[:, columns(j)],
            send_sem=two_send.at[j],
            recv_sem=two_recv.at[j],
            device_id=(c, to),
            device_id_type=MESH,
        )

    n_half = n_chunk // 2

    def project(j):
        cs = columns(j)
        product = nn(normed[...], w[:, cs])
        part[...] = product
        p[:, cs] = product.astype(bf16)
        own[:, cs] = part[slab(y), :]

    def project_step(i, carry):
        j = i
        project(j)
        relay(j, up).start()
        single(j, down, fin_up).start()
        j = i + n_half
        project(j)
        relay(j, down).start()
        single(j, up, fin_dn).start()
        return carry

    lax.fori_loop(0, n_half, project_step, 0)

    loads[3].wait()
    hops[2].wait_recv()
    hops[3].wait_recv()
    onward_up.wait_recv()
    onward_down.wait_recv()

    wide = 2 * DH

    def ng_step(i, carry):
        rs = pl.ds(pl.multiple_of(i * wide, wide), wide)
        ng[:, rs] = nt(cot[...].reshape(tok, width), w[rs, :])
        return carry

    lax.fori_loop(0, feat // wide, ng_step, 0)

    def norm_back_step(h, carry):
        hs = lanes(h)
        x = attn[:, hs]
        g = ng[:, hs] * gain[:, hs]
        a = scale[h] * (g - x * jnp.mean(g * x, axis=-1, keepdims=True))
        a = a.astype(bf16)
        ag[:, hs] = a
        gs_own[hs, :] = tn(q[:, hs], a).astype(bf16)
        return carry

    lax.fori_loop(0, heads, norm_back_step, 0)
    exchange(gs_own, gs_got, 2)

    def grad_step(h, carry):
        hs = lanes(h)
        a = ag[:, hs]
        masked = jnp.where(causal, nt(a, v[:, hs]), 0.0).astype(bf16)
        dq[:, hs] = (nn(masked, k[:, hs]) + nt(a, st_pre[hs, :])).astype(bf16)
        dk[:, hs] = tn(masked, q[:, hs])
        dv[:, hs] = tn(inner[h], a)
        return carry

    lax.fori_loop(0, heads, grad_step, 0)
    out_dq = pltpu.make_async_copy(dq, dq_hbm, out_sem.at[0])
    out_dq.start()

    exchanged(gs_own, gs_got, 2)

    def suffix_step(i, total):
        at = piece_of(n_ctx - 1 - i)
        gs_sum[at, :] = total.astype(bf16)
        return total + gs_got[at, :].astype(f32)

    lax.fori_loop(0, n_ctx, suffix_step, jnp.zeros((share, DH), f32))
    exchange(gs_sum, gs_suf, 3)

    def relay_step(i, carry):
        for j, src, to, dst in ((i, down, up, fin_dn), (i + n_half, up, down, fin_up)):
            cs = columns(j)
            relay(j, to).wait_recv()
            rel[:, cs] = (rel[:, cs].astype(f32) + p[slab(to), cs].astype(f32)).astype(bf16)
            double(j, to, dst).start()
        return carry

    lax.fori_loop(0, n_half, relay_step, 0)

    exchanged(gs_sum, gs_suf, 3)

    def last_step(h, carry):
        hs = lanes(h)
        dkb[:, hs] = (dk[:, hs] + nt(v[:, hs], gs_suf[hs, :])).astype(bf16)
        dvb[:, hs] = (dv[:, hs] + nn(k[:, hs], gs_suf[hs, :])).astype(bf16)
        return carry

    lax.fori_loop(0, heads, last_step, 0)
    out_dk = pltpu.make_async_copy(dkb, dk_hbm, out_sem.at[1])
    out_dv = pltpu.make_async_copy(dvb, dv_hbm, out_sem.at[2])
    out_dk.start()
    out_dv.start()

    def sum_step(i, carry):
        for j, to, one, two in ((i, down, fin_up, fin_dn), (i + n_half, up, fin_dn, fin_up)):
            cs = columns(j)
            single(j, to, one).wait_recv()
            double(j, to, two).wait_recv()
            lo[:, cs] = (
                own[:, cs] + (fin_dn[:, cs].astype(f32) + fin_up[:, cs].astype(f32))
            ).astype(bf16)
        return carry

    lax.fori_loop(0, n_half, sum_step, 0)
    out_lo = pltpu.make_async_copy(lo, lo_hbm, out_sem.at[3])
    out_lo.start()

    for h in (*hops, onward_up, onward_down):
        h.wait_send()

    def sent_step(j, carry):
        relay(j, up).wait_send()
        single(j, up, fin_dn).wait_send()
        double(j, up, fin_dn).wait_send()
        return carry

    lax.fori_loop(0, n_chunk, sent_step, 0)
    for out in (out_dq, out_dk, out_dv, out_lo):
        out.wait()


def per_device(n_ctx, n_head, queries, key_rows, value_rows, norm_gain, out_weight, out_cotangent):
    tok, feat = queries.shape
    rows, width = out_cotangent.shape
    heads = feat // DH
    chunk = width // 6
    n_chunk = width // chunk
    state = pltpu.VMEM((feat, DH), bf16)
    any_space = pl.BlockSpec(memory_space=pl.ANY)
    vmem = pl.BlockSpec(memory_space=pltpu.VMEM)
    dma = pltpu.SemaphoreType.DMA
    return pl.pallas_call(
        functools.partial(kernel, n_ctx, n_head, chunk),
        out_shape=(
            jax.ShapeDtypeStruct((rows, width), bf16),
            jax.ShapeDtypeStruct((tok, feat), bf16),
            jax.ShapeDtypeStruct((tok, feat), bf16),
            jax.ShapeDtypeStruct((tok, feat), bf16),
        ),
        in_specs=[any_space, any_space, any_space, vmem, any_space, any_space],
        out_specs=(any_space, any_space, any_space, any_space),
        scratch_shapes=[
            pltpu.VMEM((tok, feat), bf16),
            pltpu.VMEM((tok, feat), bf16),
            pltpu.VMEM((tok, feat), bf16),
            pltpu.VMEM((feat, width), bf16),
            pltpu.VMEM((n_head, rows, width), bf16),
            pltpu.VMEM((heads, tok, tok), bf16),
            pltpu.VMEM((tok, feat), f32),
            pltpu.VMEM((heads, tok, DH), f32),
            pltpu.VMEM((tok, feat), bf16),
            pltpu.VMEM((tok, chunk), f32),
            pltpu.VMEM((rows, width), f32),
            pltpu.VMEM((tok, width), bf16),
            pltpu.VMEM((rows, width), bf16),
            pltpu.VMEM((rows, width), bf16),
            pltpu.VMEM((rows, width), bf16),
            pltpu.VMEM((tok, feat), f32),
            pltpu.VMEM((tok, feat), bf16),
            pltpu.VMEM((tok, feat), bf16),
            pltpu.VMEM((tok, feat), f32),
            pltpu.VMEM((tok, feat), f32),
            pltpu.VMEM((tok, feat), bf16),
            pltpu.VMEM((tok, feat), bf16),
            pltpu.VMEM((rows, width), bf16),
            *[state] * 8,
            dma((5,)),
            dma((4,)),
            dma((6,)),
            dma((6,)),
            dma((4,)),
            dma((4,)),
            *[dma((n_chunk,))] * 6,
        ],
        compiler_params=pltpu.CompilerParams(
            collective_id=0, has_side_effects=True, vmem_limit_bytes=56 * 1024 * 1024
        ),
        cost_estimate=pl.CostEstimate(
            flops=8_000_000_000, bytes_accessed=18_000_000, transcendentals=0
        ),
    )(
        queries,
        key_rows,
        value_rows,
        norm_gain.reshape(1, feat),
        out_weight,
        out_cotangent,
    )


def solution(mesh):
    in_specs = (
        P("ctx", "head"),
        P("ctx", "head"),
        P("ctx", "head"),
        P("head"),
        P("head", None),
        P(("ctx", "head"), None),
    )
    out_specs = (P(("ctx", "head"), None), P("ctx", "head"), P("ctx", "head"), P("ctx", "head"))
    return jax.shard_map(
        functools.partial(per_device, mesh.shape["ctx"], mesh.shape["head"]),
        mesh=mesh,
        in_specs=in_specs,
        out_specs=out_specs,
        check_vma=False,
    )
```

time: 267 us -> 72.9 us (0.27)
  waiting for transfers between devices: 194 us -> 0 us
  Pallas kernels: 0 us -> 64.2 us
  matrix products: 49.3 us -> 0 us
  between operations: 13.9 us -> 0.64 us
  other arithmetic: 2.76 us -> 0 us
    all_gather x3 -> x0, waiting for transfers between devices: 138 us -> none  [the longest x1 53.5 us: per_device(): piece = lax.all_gather(grad_state[None], 'ctx', axis=0, tiled=True)]
    pallas_call x0 -> x1, Pallas kernels: none -> 64.2 us  [per_device(): pl.pallas_call(functools.partial(kernel, n_ctx, n_head, chunk), out_shape...]
    reduce_scatter x1 -> x0, waiting for transfers between devices: 55.3 us -> none  [per_device(): lax.psum_scatter(jnp.dot(normed, out_weight, preferred_element_type=f32),...]
    dot_general x16 -> x0, matrix products: 49.3 us -> none  [the longest x2 16.4 us: per_device(): jnp.einsum('n,nhde->hde', weights, piece, preferred_element_type=f32)]
    unnamed x14 -> x4, local copies, waits for them, and re-layouts: 4.36 us -> 7.67 us
    convert_element_type x2 -> x0, other arithmetic: 2.72 us -> none  [the longest x1 2.36 us: per_device(): layer_out = lax.psum_scatter(jnp.dot(normed, out_weight, preferred_elemen...]
  transfers between devices with their start and end apart: 4 -> 0, of which waited for: 4 -> 0; matrix products, arithmetic and copies ran while one was open for 10% -> 0% of each run, Pallas kernels for 0% -> 0%
where the time goes in v1:
time: 72.9 us; the launch traced here: 72.5 us
  Pallas kernels  64.2 us (88%)
  local copies, waits for them, and re-layouts  7.67 us (11%)
    pallas_call x1, Pallas kernels, per_device(): pl.pallas_call(functools.partial(kernel, n_ctx, n_head, chunk), out_shape...  64.2 us
    unnamed x4, local copies, waits for them, and re-layouts  7.67 us

profile of v1, /device:TPU:1, one launch (start us, length us, event | category | flops | bytes accessed | tf_op | source)
XLA Modules:
  0.0 72.5 jit_solution(15008461947148194789)
XLA Ops:
  0.6 64.2 %shard_map.93 = (bf16[64,6144]{1,0:T(8,128)(2,1)}, bf16[256,1024]{1,0:T(8,128)(2,1)}, bf16[256,1024]{1,0:T(8,128)(2,1)}, bf16[256,1024]{1,0:T(8,128)(2,1)}) custom-call(bf16[256,1024]{1,0:T(8,128)(2,1)} %q_hbm.1, bf16[256,1024]{1,0:T(8,128)(2,1)} %k_hbm.1, bf16[256,1024]{1,0:T(8,128)(2,1)} %v_hbm.1, f32[1,1024]{1,0:T(1,128)} %bitcast.1, ...), custom_call_target="tpu_custom_call" | custom-call | flops 8000000000 | bytes 18000000 | tf_op jit(solution)/shard_map/pallas_call | solution.py:404
  64.9 2.1 %copy.14 = bf16[64,6144]{1,0:T(8,128)(2,1)} copy(bf16[64,6144]{1,0:T(8,128)(2,1)} %get-tuple-element.8) | data formatting | bytes 1572864
  66.9 1.9 %copy.15 = bf16[256,1024]{1,0:T(8,128)(2,1)} copy(bf16[256,1024]{1,0:T(8,128)(2,1)} %get-tuple-element.9) | data formatting | bytes 1048576
  68.8 1.9 %copy.16 = bf16[256,1024]{1,0:T(8,128)(2,1)} copy(bf16[256,1024]{1,0:T(8,128)(2,1)} %get-tuple-element.10) | data formatting | bytes 1048576
  70.7 1.9 %copy.17 = bf16[256,1024]{1,0:T(8,128)(2,1)} copy(bf16[256,1024]{1,0:T(8,128)(2,1)} %get-tuple-element.11) | data formatting | bytes 1048576

commit v2 on v1

--- a/solution.py
+++ b/solution.py
@@ -35,10 +35,10 @@
     gain,
     w_hbm,
     cot_hbm,
-    lo_hbm,
-    dq_hbm,
-    dk_hbm,
-    dv_hbm,
+    lo,
+    dq,
+    dkb,
+    dvb,
     q,
     k,
     v,
@@ -56,12 +56,8 @@
     fin_up,
     ng,
     ag,
-    dq,
     dk,
     dv,
-    dkb,
-    dvb,
-    lo,
     st_own,
     st_got,
     st_sum,
@@ -71,7 +67,6 @@
     gs_sum,
     gs_suf,
     ld_sem,
-    out_sem,
     ag_send,
     ag_recv,
     sc_send,
@@ -326,8 +321,6 @@
         return carry
 
     lax.fori_loop(0, heads, grad_step, 0)
-    out_dq = pltpu.make_async_copy(dq, dq_hbm, out_sem.at[0])
-    out_dq.start()
 
     exchanged(gs_own, gs_got, 2)
 
@@ -358,10 +351,6 @@
         return carry
 
     lax.fori_loop(0, heads, last_step, 0)
-    out_dk = pltpu.make_async_copy(dkb, dk_hbm, out_sem.at[1])
-    out_dv = pltpu.make_async_copy(dvb, dv_hbm, out_sem.at[2])
-    out_dk.start()
-    out_dv.start()
 
     def sum_step(i, carry):
         for j, to, one, two in ((i, down, fin_up, fin_dn), (i + n_half, up, fin_dn, fin_up)):
@@ -374,8 +363,6 @@
         return carry
 
     lax.fori_loop(0, n_half, sum_step, 0)
-    out_lo = pltpu.make_async_copy(lo, lo_hbm, out_sem.at[3])
-    out_lo.start()
 
     for h in (*hops, onward_up, onward_down):
         h.wait_send()
@@ -387,8 +374,18 @@
         return carry
 
     lax.fori_loop(0, n_chunk, sent_step, 0)
-    for out in (out_dq, out_dk, out_dv, out_lo):
-        out.wait()
+
+
+def store_kernel(*refs):
+    sources, results, sem = refs[:4], refs[4:8], refs[8]
+    copies = [
+        pltpu.make_async_copy(src, dst, sem.at[i])
+        for i, (src, dst) in enumerate(zip(sources, results))
+    ]
+    for copy in copies:
+        copy.start()
+    for copy in copies:
+        copy.wait()
 
 
 def per_device(n_ctx, n_head, queries, key_rows, value_rows, norm_gain, out_weight, out_cotangent):
@@ -401,16 +398,16 @@
     any_space = pl.BlockSpec(memory_space=pl.ANY)
     vmem = pl.BlockSpec(memory_space=pltpu.VMEM)
     dma = pltpu.SemaphoreType.DMA
-    return pl.pallas_call(
+    results = pl.pallas_call(
         functools.partial(kernel, n_ctx, n_head, chunk),
         out_shape=(
-            jax.ShapeDtypeStruct((rows, width), bf16),
-            jax.ShapeDtypeStruct((tok, feat), bf16),
-            jax.ShapeDtypeStruct((tok, feat), bf16),
-            jax.ShapeDtypeStruct((tok, feat), bf16),
+            pltpu.VMEM((rows, width), bf16),
+            pltpu.VMEM((tok, feat), bf16),
+            pltpu.VMEM((tok, feat), bf16),
+            pltpu.VMEM((tok, feat), bf16),
         ),
         in_specs=[any_space, any_space, any_space, vmem, any_space, any_space],
-        out_specs=(any_space, any_space, any_space, any_space),
+        out_specs=(vmem, vmem, vmem, vmem),
         scratch_shapes=[
             pltpu.VMEM((tok, feat), bf16),
             pltpu.VMEM((tok, feat), bf16),
@@ -429,15 +426,10 @@
             pltpu.VMEM((rows, width), bf16),
             pltpu.VMEM((tok, feat), f32),
             pltpu.VMEM((tok, feat), bf16),
-            pltpu.VMEM((tok, feat), bf16),
             pltpu.VMEM((tok, feat), f32),
             pltpu.VMEM((tok, feat), f32),
-            pltpu.VMEM((tok, feat), bf16),
-            pltpu.VMEM((tok, feat), bf16),
-            pltpu.VMEM((rows, width), bf16),
             *[state] * 8,
             dma((5,)),
-            dma((4,)),
             dma((6,)),
             dma((6,)),
             dma((4,)),
@@ -445,7 +437,7 @@
             *[dma((n_chunk,))] * 6,
         ],
         compiler_params=pltpu.CompilerParams(
-            collective_id=0, has_side_effects=True, vmem_limit_bytes=56 * 1024 * 1024
+            collective_id=0, has_side_effects=True, vmem_limit_bytes=60 * 1024 * 1024
         ),
         cost_estimate=pl.CostEstimate(
             flops=8_000_000_000, bytes_accessed=18_000_000, transcendentals=0
@@ -458,6 +450,14 @@
         out_weight,
         out_cotangent,
     )
+    return pl.pallas_call(
+        store_kernel,
+        out_shape=tuple(jax.ShapeDtypeStruct(r.shape, r.dtype) for r in results),
+        in_specs=[vmem] * 4,
+        out_specs=(any_space,) * 4,
+        scratch_shapes=[dma((4,))],
+        compiler_params=pltpu.CompilerParams(vmem_limit_bytes=1024 * 1024),
+    )(*(pltpu.with_memory_space_constraint(r, pltpu.VMEM) for r in results))
 
 
 def solution(mesh):

time: 72.9 us -> 65.6 us (0.90)
  local copies, waits for them, and re-layouts: 7.67 us -> 0 us
    unnamed x4 -> x0, local copies, waits for them, and re-layouts: 7.67 us -> none
    pallas_call x0 -> x1, Pallas kernels: none -> 1.43 us  [per_device(): pl.pallas_call(store_kernel, out_shape=tuple((jax.ShapeDtypeStruct(r.shap...]
    pallas_call x1, Pallas kernels: 64.2 us -> 63.4 us  [per_device(): pl.pallas_call(functools.partial(kernel, n_ctx, n_head, chunk), out_shape...]
where the time goes in v2:
time: 65.6 us; the launch traced here: 65.4 us
  Pallas kernels  64.8 us (99%)
    pallas_call x1, Pallas kernels, per_device(): pl.pallas_call(functools.partial(kernel, n_ctx, n_head, chunk), out_shape...  63.4 us
    pallas_call x1, Pallas kernels, per_device(): pl.pallas_call(store_kernel, out_shape=tuple((jax.ShapeDtypeStruct(r.shap...  1.43 us

profile of v2, /device:TPU:1, one launch (start us, length us, event | category | flops | bytes accessed | tf_op | source)
XLA Modules:
  0.0 65.4 jit_solution(10721842611825735309)
XLA Ops:
  0.6 63.4 %shard_map.93 = (bf16[64,6144]{1,0:T(8,128)(2,1)S(1)}, bf16[256,1024]{1,0:T(8,128)(2,1)S(1)}, bf16[256,1024]{1,0:T(8,128)(2,1)S(1)}, bf16[256,1024]{1,0:T(8,128)(2,1)S(1)}) custom-call(bf16[256,1024]{1,0:T(8,128)(2,1)} %q_hbm.1, bf16[256,1024]{1,0:T(8,128)(2,1)} %k_hbm.1, bf16[256,1024]{1,0:T(8,128)(2,1)} %v_hbm.1, f32[1,1024]{1,0:T(1,128)} %bitcast.1, ...), custom_call_target="tpu_custom_call" | custom-call | flops 8000000000 | bytes 18000000 | tf_op jit(solution)/shard_map/pallas_call | solution.py:401
  64.0 1.4 %shard_map.94 = (bf16[64,6144]{1,0:T(8,128)(2,1)}, bf16[256,1024]{1,0:T(8,128)(2,1)}, bf16[256,1024]{1,0:T(8,128)(2,1)}, bf16[256,1024]{1,0:T(8,128)(2,1)}) custom-call(bf16[64,6144]{1,0:T(8,128)(2,1)S(1)} %get-tuple-element.8.refs_0_, bf16[256,1024]{1,0:T(8,128)(2,1)S(1)} %get-tuple-element.9.refs_1_, bf16[256,1024]{1,0:T(8,128)(2,1)S(1)} %get-tuple-element.10.refs_2_, ...), custom_call_target="tpu_custom_call" | custom-call | tf_op jit(solution)/shard_map/pallas_call | solution.py:453

commit v3 on v2

--- a/solution.py
+++ b/solution.py
@@ -67,6 +67,7 @@
     gs_sum,
     gs_suf,
     ld_sem,
+    ready,
     ag_send,
     ag_recv,
     sc_send,
@@ -89,6 +90,7 @@
     width = cot.shape[2]
     n_chunk = width // chunk
     half = rows // 2
+    wing = width // 2
     share = st_own.shape[0] // n_ctx
 
     loads = [
@@ -103,36 +105,46 @@
     barrier = pltpu.get_barrier_semaphore()
 
     def greet(i, carry):
-        pl.semaphore_signal(
-            barrier, inc=1, device_id=(lax.rem(c + i, n_ctx), y), device_id_type=MESH
-        )
+        pl.semaphore_signal(barrier, inc=1, device_id=(i, y), device_id_type=MESH)
+        return carry
+
+    def answer(i, carry):
+        pl.semaphore_signal(ready, inc=1, device_id=(i, y), device_id_type=MESH)
         return carry
 
     for near in (up, down):
         pl.semaphore_signal(barrier, inc=1, device_id=(c, near), device_id_type=MESH)
-    lax.fori_loop(1, n_ctx, greet, 0)
-    pl.semaphore_wait(barrier, n_ctx + 1)
-
-    first, second = pl.ds(0, half), pl.ds(half, half)
-
-    def hop(src, owner, piece, to, i):
+    lax.fori_loop(c + 1, n_ctx, greet, 0)
+    pl.semaphore_wait(barrier, c + 2)
+
+    def quarter(r, h):
+        return pl.ds(r * half, half), pl.ds(h * wing, wing)
+
+    def hop(src, owner, r, h, to, i):
         return pltpu.make_async_remote_copy(
-            src_ref=src,
-            dst_ref=cot.at[owner, piece],
+            src_ref=src.at[quarter(r, h)],
+            dst_ref=cot.at[(owner, *quarter(r, h))],
             send_sem=ag_send.at[i],
             recv_sem=ag_recv.at[i],
             device_id=(c, to),
             device_id_type=MESH,
         )
 
-    hops = [
-        hop(cot_hbm.at[first], y, first, up, 0),
-        hop(cot_hbm.at[second], y, second, down, 3),
-        hop(cot_hbm.at[second], y, second, up, 1),
-        hop(cot_hbm.at[first], y, first, down, 4),
-    ]
-    for h in hops:
-        h.start()
+    ups = [hop(cot_hbm, y, r, h, up, 2 * h + r) for h in (0, 1) for r in (0, 1)]
+    downs = [hop(cot_hbm, y, 1 - r, h, down, 4 + 2 * h + r) for h in (0, 1) for r in (0, 1)]
+    for one, other in zip(ups, downs):
+        one.start()
+        other.start()
+    lax.fori_loop(0, c, answer, 0)
+
+    def onward(h):
+        ups[2 * h].wait_recv()
+        on_up = hop(cot.at[down], down, 0, h, up, 8 + h)
+        on_up.start()
+        downs[2 * h].wait_recv()
+        on_down = hop(cot.at[up], up, 1, h, down, 10 + h)
+        on_down.start()
+        return on_up, on_down
 
     def lanes(h):
         return pl.ds(pl.multiple_of(h * DH, DH), DH)
@@ -142,7 +154,7 @@
 
     def exchange(src, dst, i):
         def step(j, carry):
-            peer = lax.rem(c + j, n_ctx)
+            peer = lax.rem(c + 1 + lax.rem(j + n_ctx // 2, n_ctx - 1), n_ctx)
             pltpu.make_async_remote_copy(
                 src_ref=src.at[piece_of(peer)],
                 dst_ref=dst.at[piece_of(c)],
@@ -178,6 +190,11 @@
         return carry
 
     lax.fori_loop(0, heads, state_step, 0)
+
+    @pl.when(c < n_ctx - 1)
+    def _():
+        pl.semaphore_wait(ready, n_ctx - 1 - c)
+
     exchange(st_own, st_got, 0)
 
     loads[2].wait()
@@ -194,6 +211,7 @@
 
     lax.fori_loop(0, heads, inner_step, 0)
 
+    onward_first = onward(0)
     exchanged(st_own, st_got, 0)
 
     def prefix_step(i, total):
@@ -202,6 +220,7 @@
 
     lax.fori_loop(0, n_ctx, prefix_step, jnp.zeros((share, DH), f32))
     exchange(st_sum, st_pre, 1)
+    onward_second = onward(1)
     exchanged(st_sum, st_pre, 1)
 
     def norm_step(h, carry):
@@ -215,13 +234,6 @@
         return carry
 
     lax.fori_loop(0, heads, norm_step, 0)
-
-    hops[0].wait_recv()
-    onward_up = hop(cot.at[down, first], down, first, up, 2)
-    onward_up.start()
-    hops[1].wait_recv()
-    onward_down = hop(cot.at[up, second], up, second, down, 5)
-    onward_down.start()
 
     loads[4].wait()
 
@@ -271,32 +283,42 @@
         own[:, cs] = part[slab(y), :]
 
     def project_step(i, carry):
-        j = i
-        project(j)
-        relay(j, up).start()
-        single(j, down, fin_up).start()
-        j = i + n_half
-        project(j)
-        relay(j, down).start()
-        single(j, up, fin_dn).start()
+        project(i)
+        relay(i, up).start()
+        project(i + n_half)
+        relay(i + n_half, down).start()
+        return carry
+
+    def single_step(i, carry):
+        single(i, down, fin_up).start()
+        single(i + n_half, up, fin_dn).start()
         return carry
 
     lax.fori_loop(0, n_half, project_step, 0)
+    lax.fori_loop(0, n_half, single_step, 0)
+
+    wide = 2 * DH
+
+    def cot_columns(h):
+        return cot[:, :, h * wing : (h + 1) * wing].reshape(tok, wing)
+
+    def ng_first(i, carry):
+        rs = pl.ds(pl.multiple_of(i * wide, wide), wide)
+        ng[:, rs] = nt(cot_columns(0), w[rs, :wing])
+        return carry
+
+    def ng_second(i, carry):
+        rs = pl.ds(pl.multiple_of(i * wide, wide), wide)
+        ng[:, rs] += nt(cot_columns(1), w[rs, wing:])
+        return carry
 
     loads[3].wait()
-    hops[2].wait_recv()
-    hops[3].wait_recv()
-    onward_up.wait_recv()
-    onward_down.wait_recv()
-
-    wide = 2 * DH
-
-    def ng_step(i, carry):
-        rs = pl.ds(pl.multiple_of(i * wide, wide), wide)
-        ng[:, rs] = nt(cot[...].reshape(tok, width), w[rs, :])
-        return carry
-
-    lax.fori_loop(0, feat // wide, ng_step, 0)
+    for h in (ups[1], downs[1], *onward_first):
+        h.wait_recv()
+    lax.fori_loop(0, feat // wide, ng_first, 0)
+    for h in (ups[3], downs[3], *onward_second):
+        h.wait_recv()
+    lax.fori_loop(0, feat // wide, ng_second, 0)
 
     def norm_back_step(h, carry):
         hs = lanes(h)
@@ -322,16 +344,6 @@
 
     lax.fori_loop(0, heads, grad_step, 0)
 
-    exchanged(gs_own, gs_got, 2)
-
-    def suffix_step(i, total):
-        at = piece_of(n_ctx - 1 - i)
-        gs_sum[at, :] = total.astype(bf16)
-        return total + gs_got[at, :].astype(f32)
-
-    lax.fori_loop(0, n_ctx, suffix_step, jnp.zeros((share, DH), f32))
-    exchange(gs_sum, gs_suf, 3)
-
     def relay_step(i, carry):
         for j, src, to, dst in ((i, down, up, fin_dn), (i + n_half, up, down, fin_up)):
             cs = columns(j)
@@ -340,8 +352,19 @@
             double(j, to, dst).start()
         return carry
 
-    lax.fori_loop(0, n_half, relay_step, 0)
-
+    lax.fori_loop(0, n_half - 1, relay_step, 0)
+
+    exchanged(gs_own, gs_got, 2)
+
+    def suffix_step(i, total):
+        at = piece_of(n_ctx - 1 - i)
+        gs_sum[at, :] = total.astype(bf16)
+        return total + gs_got[at, :].astype(f32)
+
+    lax.fori_loop(0, n_ctx, suffix_step, jnp.zeros((share, DH), f32))
+    exchange(gs_sum, gs_suf, 3)
+
+    relay_step(n_half - 1, 0)
     exchanged(gs_sum, gs_suf, 3)
 
     def last_step(h, carry):
@@ -364,7 +387,7 @@
 
     lax.fori_loop(0, n_half, sum_step, 0)
 
-    for h in (*hops, onward_up, onward_down):
+    for h in (*ups, *downs, *onward_first, *onward_second):
         h.wait_send()
 
     def sent_step(j, carry):
@@ -430,8 +453,9 @@
             pltpu.VMEM((tok, feat), f32),
             *[state] * 8,
             dma((5,)),
-            dma((6,)),
-            dma((6,)),
+            pltpu.SemaphoreType.REGULAR,
+            dma((12,)),
+            dma((12,)),
             dma((4,)),
             dma((4,)),
             *[dma((n_chunk,))] * 6,

time: 65.6 us -> 61.6 us (0.939)
  the two profiles are of different devices: /device:TPU:1 before, /device:TPU:96 now
where the time goes in v3:
time: 61.6 us; the launch traced here: 61.4 us
  Pallas kernels  60.8 us (99%)
  between operations  0.64 us (1%)
    pallas_call x1, Pallas kernels, per_device(): pl.pallas_call(functools.partial(kernel, n_ctx, n_head, chunk), out_shape...  59.4 us
    pallas_call x1, Pallas kernels, per_device(): pl.pallas_call(store_kernel, out_shape=tuple((jax.ShapeDtypeStruct(r.shap...  1.43 us

profile of v3, /device:TPU:96, one launch (start us, length us, event | category | flops | bytes accessed | tf_op | source)
XLA Modules:
  0.0 61.4 jit_solution(14190714934867549776)
XLA Ops:
  0.6 59.4 %shard_map.93 = (bf16[64,6144]{1,0:T(8,128)(2,1)S(1)}, bf16[256,1024]{1,0:T(8,128)(2,1)S(1)}, bf16[256,1024]{1,0:T(8,128)(2,1)S(1)}, bf16[256,1024]{1,0:T(8,128)(2,1)S(1)}) custom-call(bf16[256,1024]{1,0:T(8,128)(2,1)} %q_hbm.1, bf16[256,1024]{1,0:T(8,128)(2,1)} %k_hbm.1, bf16[256,1024]{1,0:T(8,128)(2,1)} %v_hbm.1, f32[1,1024]{1,0:T(1,128)} %bitcast.1, ...), custom_call_target="tpu_custom_call" | custom-call | flops 8000000000 | bytes 18000000 | tf_op jit(solution)/shard_map/pallas_call | solution.py:424
  60.0 1.4 %shard_map.94 = (bf16[64,6144]{1,0:T(8,128)(2,1)}, bf16[256,1024]{1,0:T(8,128)(2,1)}, bf16[256,1024]{1,0:T(8,128)(2,1)}, bf16[256,1024]{1,0:T(8,128)(2,1)}) custom-call(bf16[64,6144]{1,0:T(8,128)(2,1)S(1)} %get-tuple-element.8.refs_0_, bf16[256,1024]{1,0:T(8,128)(2,1)S(1)} %get-tuple-element.9.refs_1_, bf16[256,1024]{1,0:T(8,128)(2,1)S(1)} %get-tuple-element.10.refs_2_, ...), custom_call_target="tpu_custom_call" | custom-call | tf_op jit(solution)/shard_map/pallas_call | solution.py:477

commit v4 on v3

--- a/solution.py
+++ b/solution.py
@@ -8,6 +8,7 @@
 from jax.sharding import PartitionSpec as P
 
 DH = 128
+N_Z = 4
 MESH = pl.DeviceIdType.MESH
 f32 = jnp.float32
 bf16 = jnp.bfloat16
@@ -27,6 +28,7 @@
 
 def kernel(
     n_ctx,
+    n_z,
     n_head,
     chunk,
     q_hbm,
@@ -68,6 +70,7 @@
     gs_suf,
     ld_sem,
     ready,
+    here,
     ag_send,
     ag_recv,
     sc_send,
@@ -103,19 +106,33 @@
         load.start()
 
     barrier = pltpu.get_barrier_semaphore()
-
-    def greet(i, carry):
-        pl.semaphore_signal(barrier, inc=1, device_id=(i, y), device_id_type=MESH)
-        return carry
-
-    def answer(i, carry):
-        pl.semaphore_signal(ready, inc=1, device_id=(i, y), device_id_type=MESH)
+    n_group = n_ctx // n_z
+    z, g = c // n_group, c % n_group
+
+    def signal(sem, to):
+        pl.semaphore_signal(sem, inc=1, device_id=(to, y), device_id_type=MESH)
+
+    def greet_member(i, carry):
+        signal(barrier, z * n_group + i)
+        return carry
+
+    def greet_line(i, carry):
+        signal(barrier, i * n_group + g)
+        return carry
+
+    def answer_member(i, carry):
+        signal(ready, z * n_group + i)
+        return carry
+
+    def answer_line(i, carry):
+        signal(ready, i * n_group + g)
         return carry
 
     for near in (up, down):
         pl.semaphore_signal(barrier, inc=1, device_id=(c, near), device_id_type=MESH)
-    lax.fori_loop(c + 1, n_ctx, greet, 0)
-    pl.semaphore_wait(barrier, c + 2)
+    lax.fori_loop(z + 1, n_z, greet_line, 0)
+    lax.fori_loop(g + 1, n_group, greet_member, 0)
+    pl.semaphore_wait(barrier, 2 + z + g)
 
     def quarter(r, h):
         return pl.ds(r * half, half), pl.ds(h * wing, wing)
@@ -135,7 +152,8 @@
     for one, other in zip(ups, downs):
         one.start()
         other.start()
-    lax.fori_loop(0, c, answer, 0)
+    lax.fori_loop(0, z, answer_line, 0)
+    lax.fori_loop(0, g, answer_member, 0)
 
     def onward(h):
         ups[2 * h].wait_recv()
@@ -193,7 +211,14 @@
 
     @pl.when(c < n_ctx - 1)
     def _():
-        pl.semaphore_wait(ready, n_ctx - 1 - c)
+        pl.semaphore_wait(ready, n_z - 1 - z + n_group - 1 - g)
+
+    def tell_line(i, carry):
+        signal(here, lax.rem(z + i, n_z) * n_group + g)
+        return carry
+
+    lax.fori_loop(1, n_z, tell_line, 0)
+    pl.semaphore_wait(here, n_z - 1)
 
     exchange(st_own, st_got, 0)
 
@@ -411,7 +436,7 @@
         copy.wait()
 
 
-def per_device(n_ctx, n_head, queries, key_rows, value_rows, norm_gain, out_weight, out_cotangent):
+def per_device(n_ctx, n_z, n_head, queries, key_rows, value_rows, norm_gain, out_weight, out_cotangent):
     tok, feat = queries.shape
     rows, width = out_cotangent.shape
     heads = feat // DH
@@ -422,7 +447,7 @@
     vmem = pl.BlockSpec(memory_space=pltpu.VMEM)
     dma = pltpu.SemaphoreType.DMA
     results = pl.pallas_call(
-        functools.partial(kernel, n_ctx, n_head, chunk),
+        functools.partial(kernel, n_ctx, n_z, n_head, chunk),
         out_shape=(
             pltpu.VMEM((rows, width), bf16),
             pltpu.VMEM((tok, feat), bf16),
@@ -453,6 +478,7 @@
             pltpu.VMEM((tok, feat), f32),
             *[state] * 8,
             dma((5,)),
+            pltpu.SemaphoreType.REGULAR,
             pltpu.SemaphoreType.REGULAR,
             dma((12,)),
             dma((12,)),
@@ -495,7 +521,7 @@
     )
     out_specs = (P(("ctx", "head"), None), P("ctx", "head"), P("ctx", "head"), P("ctx", "head"))
     return jax.shard_map(
-        functools.partial(per_device, mesh.shape["ctx"], mesh.shape["head"]),
+        functools.partial(per_device, mesh.shape["ctx"], N_Z, mesh.shape["head"]),
         mesh=mesh,
         in_specs=in_specs,
         out_specs=out_specs,

time: 61.6 us -> 60 us (0.974)
  the two profiles are of different devices: /device:TPU:96 before, /device:TPU:1 now
where the time goes in v4:
time: 60 us; the launch traced here: 59 us
  Pallas kernels  58.4 us (97%)
  between operations  0.64 us (1%)
    pallas_call x1, Pallas kernels, per_device(): pl.pallas_call(functools.partial(kernel, n_ctx, n_z, n_head, chunk), out_...  56.9 us
    pallas_call x1, Pallas kernels, per_device(): pl.pallas_call(store_kernel, out_shape=tuple((jax.ShapeDtypeStruct(r.shap...  1.43 us

profile of v4, /device:TPU:1, one launch (start us, length us, event | category | flops | bytes accessed | tf_op | source)
XLA Modules:
  0.0 59.0 jit_solution(8102622809459922161)
XLA Ops:
  0.6 56.9 %shard_map.93 = (bf16[64,6144]{1,0:T(8,128)(2,1)S(1)}, bf16[256,1024]{1,0:T(8,128)(2,1)S(1)}, bf16[256,1024]{1,0:T(8,128)(2,1)S(1)}, bf16[256,1024]{1,0:T(8,128)(2,1)S(1)}) custom-call(bf16[256,1024]{1,0:T(8,128)(2,1)} %q_hbm.1, bf16[256,1024]{1,0:T(8,128)(2,1)} %k_hbm.1, bf16[256,1024]{1,0:T(8,128)(2,1)} %v_hbm.1, f32[1,1024]{1,0:T(1,128)} %bitcast.1, ...), custom_call_target="tpu_custom_call" | custom-call | flops 8000000000 | bytes 18000000 | tf_op jit(solution)/shard_map/pallas_call | solution.py:449
  57.6 1.4 %shard_map.94 = (bf16[64,6144]{1,0:T(8,128)(2,1)}, bf16[256,1024]{1,0:T(8,128)(2,1)}, bf16[256,1024]{1,0:T(8,128)(2,1)}, bf16[256,1024]{1,0:T(8,128)(2,1)}) custom-call(bf16[64,6144]{1,0:T(8,128)(2,1)S(1)} %get-tuple-element.8.refs_0_, bf16[256,1024]{1,0:T(8,128)(2,1)S(1)} %get-tuple-element.9.refs_1_, bf16[256,1024]{1,0:T(8,128)(2,1)S(1)} %get-tuple-element.10.refs_2_, ...), custom_call_target="tpu_custom_call" | custom-call | tf_op jit(solution)/shard_map/pallas_call | solution.py:503

commit v5 on v4

--- a/solution.py
+++ b/solution.py
@@ -8,6 +8,7 @@
 from jax.sharding import PartitionSpec as P
 
 DH = 128
+N_STORE = 4
 N_Z = 4
 MESH = pl.DeviceIdType.MESH
 f32 = jnp.float32
@@ -102,18 +103,21 @@
             ((k_hbm, k), (v_hbm, v), (q_hbm, q), (cot_hbm, cot.at[y]), (w_hbm, w))
         )
     ]
-    for load in loads:
-        load.start()
-
     barrier = pltpu.get_barrier_semaphore()
     n_group = n_ctx // n_z
     z, g = c // n_group, c % n_group
 
+    def ranked(i):
+        x = i // 2
+        return 2 * (x + (x // 2) * (1 - 2 * (x % 2))) + i % 2
+
+    rank = ranked(g)
+
     def signal(sem, to):
         pl.semaphore_signal(sem, inc=1, device_id=(to, y), device_id_type=MESH)
 
     def greet_member(i, carry):
-        signal(barrier, z * n_group + i)
+        signal(barrier, z * n_group + ranked(i))
         return carry
 
     def greet_line(i, carry):
@@ -121,7 +125,7 @@
         return carry
 
     def answer_member(i, carry):
-        signal(ready, z * n_group + i)
+        signal(ready, z * n_group + ranked(i))
         return carry
 
     def answer_line(i, carry):
@@ -131,36 +135,41 @@
     for near in (up, down):
         pl.semaphore_signal(barrier, inc=1, device_id=(c, near), device_id_type=MESH)
     lax.fori_loop(z + 1, n_z, greet_line, 0)
-    lax.fori_loop(g + 1, n_group, greet_member, 0)
-    pl.semaphore_wait(barrier, 2 + z + g)
-
-    def quarter(r, h):
-        return pl.ds(r * half, half), pl.ds(h * wing, wing)
+    lax.fori_loop(rank + 1, n_group, greet_member, 0)
+    for i in (3, 0, 1, 2, 4):
+        loads[i].start()
+    loads[3].wait()
+    pl.semaphore_wait(barrier, 2 + z + rank)
+
+    def portion(r, h):
+        return pl.ds(*r), pl.ds(h * wing, wing)
+
+    every, upper, lower = (0, rows), (0, half), (half, half)
 
     def hop(src, owner, r, h, to, i):
         return pltpu.make_async_remote_copy(
-            src_ref=src.at[quarter(r, h)],
-            dst_ref=cot.at[(owner, *quarter(r, h))],
+            src_ref=src.at[portion(r, h)],
+            dst_ref=cot.at[(owner, *portion(r, h))],
             send_sem=ag_send.at[i],
             recv_sem=ag_recv.at[i],
             device_id=(c, to),
             device_id_type=MESH,
         )
 
-    ups = [hop(cot_hbm, y, r, h, up, 2 * h + r) for h in (0, 1) for r in (0, 1)]
-    downs = [hop(cot_hbm, y, 1 - r, h, down, 4 + 2 * h + r) for h in (0, 1) for r in (0, 1)]
+    ups = [hop(cot.at[y], y, every, h, up, h) for h in (0, 1)]
+    downs = [hop(cot.at[y], y, every, h, down, 2 + h) for h in (0, 1)]
     for one, other in zip(ups, downs):
         one.start()
         other.start()
     lax.fori_loop(0, z, answer_line, 0)
-    lax.fori_loop(0, g, answer_member, 0)
+    lax.fori_loop(0, rank, answer_member, 0)
 
     def onward(h):
-        ups[2 * h].wait_recv()
-        on_up = hop(cot.at[down], down, 0, h, up, 8 + h)
+        ups[h].wait_recv()
+        on_up = hop(cot.at[down], down, upper, h, up, 4 + h)
         on_up.start()
-        downs[2 * h].wait_recv()
-        on_down = hop(cot.at[up], up, 1, h, down, 10 + h)
+        downs[h].wait_recv()
+        on_down = hop(cot.at[up], up, lower, h, down, 6 + h)
         on_down.start()
         return on_up, on_down
 
@@ -209,9 +218,9 @@
 
     lax.fori_loop(0, heads, state_step, 0)
 
-    @pl.when(c < n_ctx - 1)
+    @pl.when(n_z - 1 - z + n_group - 1 - rank > 0)
     def _():
-        pl.semaphore_wait(ready, n_z - 1 - z + n_group - 1 - g)
+        pl.semaphore_wait(ready, n_z - 1 - z + n_group - 1 - rank)
 
     def tell_line(i, carry):
         signal(here, lax.rem(z + i, n_z) * n_group + g)
@@ -278,12 +287,13 @@
             device_id_type=MESH,
         )
 
-    def single(j, to, dst):
+    def single(h, to, dst):
+        cs = pl.ds(h * wing, wing)
         return pltpu.make_async_remote_copy(
-            src_ref=p.at[slab(to), columns(j)],
-            dst_ref=dst.at[:, columns(j)],
-            send_sem=one_send.at[j],
-            recv_sem=one_recv.at[j],
+            src_ref=p.at[slab(to), cs],
+            dst_ref=dst.at[:, cs],
+            send_sem=one_send.at[h],
+            recv_sem=one_recv.at[h],
             device_id=(c, to),
             device_id_type=MESH,
         )
@@ -314,13 +324,9 @@
         relay(i + n_half, down).start()
         return carry
 
-    def single_step(i, carry):
-        single(i, down, fin_up).start()
-        single(i + n_half, up, fin_dn).start()
-        return carry
-
     lax.fori_loop(0, n_half, project_step, 0)
-    lax.fori_loop(0, n_half, single_step, 0)
+    single(0, down, fin_up).start()
+    single(1, up, fin_dn).start()
 
     wide = 2 * DH
 
@@ -337,11 +343,10 @@
         ng[:, rs] += nt(cot_columns(1), w[rs, wing:])
         return carry
 
-    loads[3].wait()
-    for h in (ups[1], downs[1], *onward_first):
+    for h in onward_first:
         h.wait_recv()
     lax.fori_loop(0, feat // wide, ng_first, 0)
-    for h in (ups[3], downs[3], *onward_second):
+    for h in onward_second:
         h.wait_recv()
     lax.fori_loop(0, feat // wide, ng_second, 0)
 
@@ -401,23 +406,26 @@
     lax.fori_loop(0, heads, last_step, 0)
 
     def sum_step(i, carry):
-        for j, to, one, two in ((i, down, fin_up, fin_dn), (i + n_half, up, fin_dn, fin_up)):
+        for j, to, two in ((i, down, fin_dn), (i + n_half, up, fin_up)):
             cs = columns(j)
-            single(j, to, one).wait_recv()
             double(j, to, two).wait_recv()
             lo[:, cs] = (
                 own[:, cs] + (fin_dn[:, cs].astype(f32) + fin_up[:, cs].astype(f32))
             ).astype(bf16)
         return carry
 
+    single(0, down, fin_up).wait_recv()
+    single(1, up, fin_dn).wait_recv()
     lax.fori_loop(0, n_half, sum_step, 0)
 
     for h in (*ups, *downs, *onward_first, *onward_second):
         h.wait_send()
 
+    single(0, down, fin_up).wait_send()
+    single(1, up, fin_dn).wait_send()
+
     def sent_step(j, carry):
         relay(j, up).wait_send()
-        single(j, up, fin_dn).wait_send()
         double(j, up, fin_dn).wait_send()
         return carry
 
@@ -426,10 +434,13 @@
 
 def store_kernel(*refs):
     sources, results, sem = refs[:4], refs[4:8], refs[8]
-    copies = [
-        pltpu.make_async_copy(src, dst, sem.at[i])
-        for i, (src, dst) in enumerate(zip(sources, results))
-    ]
+    copies = []
+    for src, dst in zip(sources, results):
+        step = src.shape[0] // N_STORE
+        for piece in (pl.ds(i * step, step) for i in range(N_STORE)):
+            copies.append(
+                pltpu.make_async_copy(src.at[piece], dst.at[piece], sem.at[len(copies)])
+            )
     for copy in copies:
         copy.start()
     for copy in copies:
@@ -480,8 +491,8 @@
             dma((5,)),
             pltpu.SemaphoreType.REGULAR,
             pltpu.SemaphoreType.REGULAR,
-            dma((12,)),
-            dma((12,)),
+            dma((8,)),
+            dma((8,)),
             dma((4,)),
             dma((4,)),
             *[dma((n_chunk,))] * 6,
@@ -505,7 +516,7 @@
         out_shape=tuple(jax.ShapeDtypeStruct(r.shape, r.dtype) for r in results),
         in_specs=[vmem] * 4,
         out_specs=(any_space,) * 4,
-        scratch_shapes=[dma((4,))],
+        scratch_shapes=[dma((4 * N_STORE,))],
         compiler_params=pltpu.CompilerParams(vmem_limit_bytes=1024 * 1024),
     )(*(pltpu.with_memory_space_constraint(r, pltpu.VMEM) for r in results))
 

time: 60 us -> 59.8 us (level); the launches traced: 59 us -> 59.5 us
  no operation moved by 1% of the time
where the time goes in v5:
time: 59.8 us; the launch traced here: 59.5 us
  Pallas kernels  58.9 us (98%)
  between operations  0.64 us (1%)
    pallas_call x1, Pallas kernels, per_device(): pl.pallas_call(functools.partial(kernel, n_ctx, n_z, n_head, chunk), out_...  57.4 us
    pallas_call x1, Pallas kernels, per_device(): pl.pallas_call(store_kernel, out_shape=tuple((jax.ShapeDtypeStruct(r.shap...  1.53 us

profile of v5, /device:TPU:1, one launch (start us, length us, event | category | flops | bytes accessed | tf_op | source)
XLA Modules:
  0.0 59.5 jit_solution(15998365616348202950)
XLA Ops:
  0.6 57.4 %shard_map.93 = (bf16[64,6144]{1,0:T(8,128)(2,1)S(1)}, bf16[256,1024]{1,0:T(8,128)(2,1)S(1)}, bf16[256,1024]{1,0:T(8,128)(2,1)S(1)}, bf16[256,1024]{1,0:T(8,128)(2,1)S(1)}) custom-call(bf16[256,1024]{1,0:T(8,128)(2,1)} %q_hbm.1, bf16[256,1024]{1,0:T(8,128)(2,1)} %k_hbm.1, bf16[256,1024]{1,0:T(8,128)(2,1)} %v_hbm.1, f32[1,1024]{1,0:T(1,128)} %bitcast.1, ...), custom_call_target="tpu_custom_call" | custom-call | flops 8000000000 | bytes 18000000 | tf_op jit(solution)/shard_map/pallas_call | solution.py:460
  58.0 1.5 %shard_map.94 = (bf16[64,6144]{1,0:T(8,128)(2,1)}, bf16[256,1024]{1,0:T(8,128)(2,1)}, bf16[256,1024]{1,0:T(8,128)(2,1)}, bf16[256,1024]{1,0:T(8,128)(2,1)}) custom-call(bf16[64,6144]{1,0:T(8,128)(2,1)S(1)} %get-tuple-element.8.refs_0_, bf16[256,1024]{1,0:T(8,128)(2,1)S(1)} %get-tuple-element.9.refs_1_, bf16[256,1024]{1,0:T(8,128)(2,1)S(1)} %get-tuple-element.10.refs_2_, ...), custom_call_target="tpu_custom_call" | custom-call | tf_op jit(solution)/shard_map/pallas_call | solution.py:514

commit v6 on v5

--- a/solution.py
+++ b/solution.py
@@ -451,7 +451,7 @@
     tok, feat = queries.shape
     rows, width = out_cotangent.shape
     heads = feat // DH
-    chunk = width // 6
+    chunk = width // 4
     n_chunk = width // chunk
     state = pltpu.VMEM((feat, DH), bf16)
     any_space = pl.BlockSpec(memory_space=pl.ANY)

time: 59.8 us -> 59.9 us (level)
  no operation moved by 1% of the time
where the time goes in v6:
time: 59.9 us; the launch traced here: 59.8 us
  Pallas kernels  59.1 us (99%)
  between operations  0.64 us (1%)
    pallas_call x1, Pallas kernels, per_device(): pl.pallas_call(functools.partial(kernel, n_ctx, n_z, n_head, chunk), out_...  57.6 us
    pallas_call x1, Pallas kernels, per_device(): pl.pallas_call(store_kernel, out_shape=tuple((jax.ShapeDtypeStruct(r.shap...  1.53 us

profile of v6, /device:TPU:1, one launch (start us, length us, event | category | flops | bytes accessed | tf_op | source)
XLA Modules:
  0.0 59.8 jit_solution(15633192083461881509)
XLA Ops:
  0.6 57.6 %shard_map.93 = (bf16[64,6144]{1,0:T(8,128)(2,1)S(1)}, bf16[256,1024]{1,0:T(8,128)(2,1)S(1)}, bf16[256,1024]{1,0:T(8,128)(2,1)S(1)}, bf16[256,1024]{1,0:T(8,128)(2,1)S(1)}) custom-call(bf16[256,1024]{1,0:T(8,128)(2,1)} %q_hbm.1, bf16[256,1024]{1,0:T(8,128)(2,1)} %k_hbm.1, bf16[256,1024]{1,0:T(8,128)(2,1)} %v_hbm.1, f32[1,1024]{1,0:T(1,128)} %bitcast.1, ...), custom_call_target="tpu_custom_call" | custom-call | flops 8000000000 | bytes 18000000 | tf_op jit(solution)/shard_map/pallas_call | solution.py:460
  58.2 1.5 %shard_map.94 = (bf16[64,6144]{1,0:T(8,128)(2,1)}, bf16[256,1024]{1,0:T(8,128)(2,1)}, bf16[256,1024]{1,0:T(8,128)(2,1)}, bf16[256,1024]{1,0:T(8,128)(2,1)}) custom-call(bf16[64,6144]{1,0:T(8,128)(2,1)S(1)} %get-tuple-element.8.refs_0_, bf16[256,1024]{1,0:T(8,128)(2,1)S(1)} %get-tuple-element.9.refs_1_, bf16[256,1024]{1,0:T(8,128)(2,1)S(1)} %get-tuple-element.10.refs_2_, ...), custom_call_target="tpu_custom_call" | custom-call | tf_op jit(solution)/shard_map/pallas_call | solution.py:514

commit v7 on v6

--- a/solution.py
+++ b/solution.py
@@ -451,7 +451,7 @@
     tok, feat = queries.shape
     rows, width = out_cotangent.shape
     heads = feat // DH
-    chunk = width // 4
+    chunk = width // 12
     n_chunk = width // chunk
     state = pltpu.VMEM((feat, DH), bf16)
     any_space = pl.BlockSpec(memory_space=pl.ANY)

time: 59.9 us -> 60.1 us (level)
  no operation moved by 1% of the time
where the time goes in v7:
time: 60.1 us; the launch traced here: 59.7 us
  Pallas kernels  59 us (98%)
  between operations  0.64 us (1%)
    pallas_call x1, Pallas kernels, per_device(): pl.pallas_call(functools.partial(kernel, n_ctx, n_z, n_head, chunk), out_...  57.5 us
    pallas_call x1, Pallas kernels, per_device(): pl.pallas_call(store_kernel, out_shape=tuple((jax.ShapeDtypeStruct(r.shap...  1.53 us

profile of v7, /device:TPU:1, one launch (start us, length us, event | category | flops | bytes accessed | tf_op | source)
XLA Modules:
  0.0 59.7 jit_solution(366373837319722229)
XLA Ops:
  0.6 57.5 %shard_map.93 = (bf16[64,6144]{1,0:T(8,128)(2,1)S(1)}, bf16[256,1024]{1,0:T(8,128)(2,1)S(1)}, bf16[256,1024]{1,0:T(8,128)(2,1)S(1)}, bf16[256,1024]{1,0:T(8,128)(2,1)S(1)}) custom-call(bf16[256,1024]{1,0:T(8,128)(2,1)} %q_hbm.1, bf16[256,1024]{1,0:T(8,128)(2,1)} %k_hbm.1, bf16[256,1024]{1,0:T(8,128)(2,1)} %v_hbm.1, f32[1,1024]{1,0:T(1,128)} %bitcast.1, ...), custom_call_target="tpu_custom_call" | custom-call | flops 8000000000 | bytes 18000000 | tf_op jit(solution)/shard_map/pallas_call | solution.py:460
  58.1 1.5 %shard_map.94 = (bf16[64,6144]{1,0:T(8,128)(2,1)}, bf16[256,1024]{1,0:T(8,128)(2,1)}, bf16[256,1024]{1,0:T(8,128)(2,1)}, bf16[256,1024]{1,0:T(8,128)(2,1)}) custom-call(bf16[64,6144]{1,0:T(8,128)(2,1)S(1)} %get-tuple-element.8.refs_0_, bf16[256,1024]{1,0:T(8,128)(2,1)S(1)} %get-tuple-element.9.refs_1_, bf16[256,1024]{1,0:T(8,128)(2,1)S(1)} %get-tuple-element.10.refs_2_, ...), custom_call_target="tpu_custom_call" | custom-call | tf_op jit(solution)/shard_map/pallas_call | solution.py:514
